TPU v7x, 32 devices: a whole 2x2x4 slice. The times are simulated.
32 devices in a mesh: pool: 2 (over x), row: 8 (over z, y), col: 2 (over core).
Axes of the slice: x: 2, y: 2, z: 4, core: 2. Of those that a mesh axis runs over, the one named last changes fastest.
Arguments:
- grad_slots: bfloat16 [48, 256, 14336], P(('pool', 'row'), 'col'), parts along dimension 0, may hold values from -6 to 6
- block_owner: int32 [32], P('pool'), parts along dimension 0, may hold values from 0 to 7, as said below
- factor: bfloat16 [8192, 4096], P(('pool', 'col'), 'row'), parts along dimension 0, may hold values from -0.125 to 0.125
- pattern: int32 [16, 8], P('pool'), parts along dimension 0, may hold values from 0 to 1, as said below
Outputs:
- precond: bfloat16 [8192, 14336], P(('pool', 'col'), 'row'), parts along dimension 0
There are 2 independent parts, one for each index of `pool`. A program takes and returns all parts, laid end to end along the dimension named above; each array names one. Nothing has to cross between parts.
Inputs may be any that keep to these rules, and one draw needn't show every extreme that they name: `block_owner`: no trainer shard holds more than 3 blocks and one holds exactly 3; a shard keeps its blocks in its first slots in increasing block order, and the other slots are unused. `pattern`: 1 on the diagonal and 0 below it.
All inputs are finite; a program needn't handle non-finite values.
Results may differ from a plain program's by a relative error of at most 0.004.
Values may be sent and summed in bfloat16 or wider, within the bound.
A program may use at most 192 MiB of HBM per device.

v0:
```python
import jax
import jax.numpy as jnp
from jax import lax
from jax.sharding import PartitionSpec as P


def body(grad_slots, block_owner, factor, pattern):
    row_idx = lax.axis_index("row")
    col_idx = lax.axis_index("col")
    slot_cap = grad_slots.shape[0]
    block_total = block_owner.shape[0]
    received = lax.all_to_all(grad_slots, "row", split_axis=2, concat_axis=0, tiled=True)
    same_owner = block_owner[:, None] == block_owner[None, :]
    earlier = jnp.arange(block_total)[None, :] < jnp.arange(block_total)[:, None]
    owner_rank = jnp.sum(same_owner & earlier, axis=1)
    slot_of = block_owner * slot_cap + owner_rank
    picked = jnp.take(received, slot_of, axis=0)
    blocks = lax.all_gather(picked, "col", axis=1, tiled=True)
    grad_cols = blocks.reshape(-1, blocks.shape[2])
    half_rows, piece_width = factor.shape
    block_count = pattern.shape[0]
    total_rows = 2 * half_rows
    block_size = total_rows // block_count
    half_blocks = block_count // 2
    col_block = (row_idx * piece_width + jnp.arange(piece_width)) // block_size
    row_blocks = col_idx * half_blocks + jnp.arange(half_blocks)
    sel_cols = (jnp.arange(block_count)[:, None] == col_block[None, :]).astype(jnp.float32)
    pattern_cols = jnp.dot(pattern.astype(jnp.float32), sel_cols)
    sel_rows = (row_blocks[:, None] == jnp.arange(block_count)[None, :]).astype(jnp.float32)
    block_mask = jnp.dot(sel_rows, pattern_cols)
    keep_mask = block_mask > 0.5
    shaped = factor.reshape(half_blocks, block_size, piece_width)
    masked = jnp.where(keep_mask[:, None, :], shaped, jnp.zeros_like(shaped)).reshape(
        half_rows, piece_width
    )
    result = jnp.dot(
        lax.all_gather(masked, "row", axis=1, tiled=True),
        grad_cols,
        preferred_element_type=jnp.float32,
    )
    return result.astype(jnp.bfloat16)


def solution(mesh):
    placed = (
        P(("pool", "row"), "col", None),
        P("pool"),
        P(("pool", "col"), "row"),
        P("pool", None),
    )
    return jax.shard_map(
        body, mesh=mesh, in_specs=placed, out_specs=P(("pool", "col"), "row"), check_vma=False
    )
```

profile of v0, /device:TPU:0, one launch (start us, length us, event | category | flops | bytes accessed | tf_op | source)
XLA Modules:
  0.0 657.5 jit_solution(4763586861439865328)
XLA Ops:
  6.5 0.0 all-gather.3.cloned.1.call-start
  6.6 0.9 fusion.3
  7.5 3.1 bitcast_select_fusion
  10.6 0.0 all-gather.3.cloned.1.call-update
  10.6 22.4 %copy.10 = bf16[3,128,14336]{1,0,2:T(4,128)(2,1)} copy(bf16[3,128,14336]{2,1,0:T(8,128)(2,1)} %param.4) | data formatting | bytes 22020096 | tf_op args[0]
  33.0 0.0 copy-start
  33.0 7.4 %all-to-all-start = ((bf16[3,128,14336]{1,0,2:T(4,128)(2,1)}), bf16[3,128,14336]{1,0,2:T(4,128)(2,1)}, u32[]{:S(2)}, u32[]{:S(2)}) async-start(bf16[3,128,14336]{1,0,2:T(4,128)(2,1)} %copy.10), calls=%async_computation | async-start | bytes 29360128 | tf_op jit(solution)/shard_map/all_to_all | solution.py:12
  40.4 0.0 all-gather.5.cloned.1.call-start
  40.5 0.0 copy-done
  40.5 0.2 convert_reduce_fusion
  40.7 504.1 %all-to-all-done = bf16[3,128,14336]{1,0,2:T(4,128)(2,1)} async-done(((bf16[3,128,14336]{1,0,2:T(4,128)(2,1)}), bf16[3,128,14336]{1,0,2:T(4,128)(2,1)}, u32[]{:S(2)}, u32[]{:S(2)}) %all-to-all-start) | async-done | bytes 11010080 | tf_op jit(solution)/shard_map/all_to_all | solution.py:12
  544.8 12.4 %copy.11 = bf16[3,128,14336]{1,2,0:T(8,128)(2,1)} copy(bf16[3,128,14336]{1,0,2:T(4,128)(2,1)} %all-to-all-done) | data formatting | bytes 22020096 | tf_op jit(solution)/shard_map/all_to_all | solution.py:12
  557.2 14.2 %copy.12 = bf16[8,3,128,1792]{3,2,1,0:T(8,128)(2,1)} copy(bf16[8,3,128,1792]{2,3,0,1:T(8,128)(2,1)} %bitcast.9) | data formatting | bytes 22020096 | tf_op jit(solution)/shard_map/all_to_all | solution.py:12
  571.3 8.2 %gather_fusion = bf16[16,128,1792]{2,1,0:T(8,128)(2,1)} fusion(bf16[24,128,1792]{2,1,0:T(8,128)(2,1)} %bitcast.10, s32[1024]{0:T(1024)S(1)} %pad_clamp_fusion), kind=kCustom, calls=%fused_computation | custom fusion | bytes 14680128 | tf_op jit(solution)/shard_map/jit(_take)/gather | solution.py:17
  579.5 6.9 %broadcast_select_fusion = bf16[16,128,1792]{2,1,0:T(8,128)(2,1)} fusion(bf16[16,128,1792]{2,1,0:T(8,128)(2,1)} %gather_fusion, pred[16]{0:T(512)(128)(4,1)S(1)} %get-tuple-element.5), kind=kLoop, calls=%fused_computation.2 | loop fusion | flops 3670016 | bytes 14680080 | tf_op jit(solution)/shard_map/jit(_take)/select_n | solution.py:17
  586.4 0.0 all-gather.5.cloned.1.call-update
  586.5 0.0 all-gather.3.cloned.1.call-done
  586.5 25.5 %all-gather.5.cloned.1.call-done = bf16[16,256,1792]{2,1,0:T(8,128)(2,1)} async-done(((bf16[16,128,1792]{2,1,0:T(8,128)(2,1)}), bf16[16,256,1792]{2,1,0:T(8,128)(2,1)}) %all-gather.5.cloned.1.call-update) | async-done | bytes 14680080 | tf_op jit(solution)/shard_map/all_gather | solution.py:18
  612.0 38.6 %convolution_convert_fusion = bf16[2048,1792]{1,0:T(8,128)(2,1)} fusion(bf16[2048,4096]{1,0:T(8,128)(2,1)} %all-gather.3.cloned.1.call-done, bf16[4096,1792]{1,0:T(8,128)(2,1)} %bitcast.11), kind=kOutput, calls=%fused_computation.1 | convolution fusion | flops 30068441088 | bytes 38797312 | tf_op jit(solution)/shard_map/dot_general | solution.py:36
  (4 shorter events, 0.0 us)
Async XLA Ops:
  6.5 579.9 %all-gather.3.cloned.1.call-start = ((), (), s32[]{:S(2)}) async-start(), calls=%async_computation.1 | async-start | bytes 18874368 | tf_op jit(solution)/shard_map/all_gather | solution.py:37
  33.0 7.5 %copy-start = (s32[16]{0:T(128)S(1)}, s32[16]{0:T(128)}, u32[]{:S(2)}) copy-start(s32[16]{0:T(128)} %param.5) | copy-start | bytes 196
  33.0 511.8 %all-to-all-start = ((bf16[3,128,14336]{1,0,2:T(4,128)(2,1)}), bf16[3,128,14336]{1,0,2:T(4,128)(2,1)}, u32[]{:S(2)}, u32[]{:S(2)}) async-start(bf16[3,128,14336]{1,0,2:T(4,128)(2,1)} %copy.10), calls=%async_computation | async-start | bytes 29360128 | tf_op jit(solution)/shard_map/all_to_all | solution.py:12
  40.4 571.6 %all-gather.5.cloned.1.call-start = ((), (), s32[]{:S(2)}) async-start(), calls=%async_computation.2 | async-start | bytes 22020096 | tf_op jit(solution)/shard_map/all_gather | solution.py:18
Sparse Core Ops, SparseCore 0:
  10.7 526.6 all-gather.2
  586.6 25.3 all-gather.4
where the time goes:
time: 659 us; the launch traced here: 657 us
  waiting for transfers between devices  530 us (80%)
  local copies, waits for them, and re-layouts  57.2 us (9%)
  matrix products  39.5 us (6%)
  between operations  13.4 us (2%)
  other arithmetic  10.2 us (2%)
  starting transfers between devices  7.44 us (1%)
    all_to_all x1, waiting for transfers between devices, body(): lax.all_to_all(grad_slots, 'row', split_axis=2, concat_axis=0, tiled=True)  504 us
    dot_general x1, matrix products, body(): jnp.dot(lax.all_gather(masked, 'row', axis=1, tiled=True), grad_cols, pre...  38.6 us
    all_to_all x2, local copies, waits for them, and re-layouts, body(): lax.all_to_all(grad_slots, 'row', split_axis=2, concat_axis=0, tiled=True)  26.6 us
    all_gather x1, waiting for transfers between devices, body(): blocks = lax.all_gather(picked, 'col', axis=1, tiled=True)  25.5 us
    unnamed x3, local copies, waits for them, and re-layouts  22.4 us
  transfers between devices with their start and end apart: 3, of which 2 were waited for; matrix products, arithmetic and copies ran while one was open for 10% of the time, Pallas kernels for 0%

commit v1 on v0

--- a/solution.py
+++ b/solution.py
@@ -9,7 +9,12 @@
     col_idx = lax.axis_index("col")
     slot_cap = grad_slots.shape[0]
     block_total = block_owner.shape[0]
-    received = lax.all_to_all(grad_slots, "row", split_axis=2, concat_axis=0, tiled=True)
+    received = jnp.concatenate(
+        lax.all_to_all(
+            jnp.stack(jnp.split(grad_slots, lax.axis_size("row"), 2), axis=0), "row", 0, 0
+        ),
+        0,
+    )
     same_owner = block_owner[:, None] == block_owner[None, :]
     earlier = jnp.arange(block_total)[None, :] < jnp.arange(block_total)[:, None]
     owner_rank = jnp.sum(same_owner & earlier, axis=1)

time: 659 us -> 545 us (0.83)
  waiting for transfers between devices: 530 us -> 444 us
  local copies, waits for them, and re-layouts: 57.2 us -> 28.8 us
    all_to_all x1, waiting for transfers between devices: 504 us -> 418 us  [body(): lax.all_to_all(jnp.stack(jnp.split(grad_slots, lax.axis_size('row'), 2),...]
    all_to_all x2 -> x0, local copies, waits for them, and re-layouts: 26.6 us -> none  [body(): lax.all_to_all(grad_slots, 'row', split_axis=2, concat_axis=0, tiled=True)]
    unnamed x3 -> x9, local copies, waits for them, and re-layouts: 22.4 us -> 18.1 us
  transfers between devices with their start and end apart: 3 -> 3, of which waited for: 2 -> 2; matrix products, arithmetic and copies ran while one was open for 10% -> 7% of each run, Pallas kernels for 0% -> 0%
where the time goes in v1:
time: 545 us; the launch traced here: 544 us
  waiting for transfers between devices  444 us (81%)
  matrix products  39.7 us (7%)
  local copies, waits for them, and re-layouts  28.8 us (5%)
  between operations  13.4 us (2%)
  other arithmetic  10.2 us (2%)
  starting transfers between devices  7.58 us (1%)
    all_to_all x1, waiting for transfers between devices, body(): lax.all_to_all(jnp.stack(jnp.split(grad_slots, lax.axis_size('row'), 2),...  418 us
    dot_general x1, matrix products, body(): jnp.dot(lax.all_gather(masked, 'row', axis=1, tiled=True), grad_cols, pre...  38.6 us
    all_gather x1, waiting for transfers between devices, body(): blocks = lax.all_gather(picked, 'col', axis=1, tiled=True)  26.6 us
    unnamed x9, local copies, waits for them, and re-layouts  18.1 us
  transfers between devices with their start and end apart: 3, of which 2 were waited for; matrix products, arithmetic and copies ran while one was open for 7% of the time, Pallas kernels for 0%

profile of v1, /device:TPU:0, one launch (start us, length us, event | category | flops | bytes accessed | tf_op | source)
XLA Modules:
  0.0 544.0 jit_solution(7315585157311805758)
XLA Ops:
  6.5 0.0 all-gather.3.cloned.1.call-start
  6.6 1.1 fusion.3
  7.7 3.1 bitcast_select_fusion
  10.7 0.0 all-gather.3.cloned.1.call-update
  10.7 2.5 bitcast_dynamic-update-slice_fusion.7
  13.3 2.6 bitcast_dynamic-update-slice_fusion.6
  15.8 2.5 bitcast_dynamic-update-slice_fusion.5
  18.4 2.5 bitcast_dynamic-update-slice_fusion.4
  20.9 2.8 bitcast_dynamic-update-slice_fusion.3
  23.6 2.6 bitcast_dynamic-update-slice_fusion.2
  26.2 2.6 bitcast_dynamic-update-slice_fusion.1
  28.8 2.5 bitcast_dynamic-update-slice_fusion
  31.3 0.0 copy-start
  31.3 7.5 %all-to-all-start = ((bf16[8,3,128,1792]{3,2,1,0:T(8,128)(2,1)}), bf16[8,3,128,1792]{3,2,1,0:T(8,128)(2,1)}, u32[]{:S(2)}, u32[]{:S(2)}) async-start(bf16[8,3,128,1792]{3,2,1,0:T(8,128)(2,1)} %bitcast_dynamic-update-slice_fusion), calls=%async_computation | async-start | bytes 22020096 | tf_op jit(solution)/shard_map/all_to_all | solution.py:13
  38.9 0.0 all-gather.5.cloned.1.call-start
  38.9 0.0 copy-done
  38.9 0.2 convert_reduce_fusion
  39.1 417.6 %all-to-all-done = bf16[8,3,128,1792]{3,2,1,0:T(8,128)(2,1)} async-done(((bf16[8,3,128,1792]{3,2,1,0:T(8,128)(2,1)}), bf16[8,3,128,1792]{3,2,1,0:T(8,128)(2,1)}, u32[]{:S(2)}, u32[]{:S(2)}) %all-to-all-start) | async-done | bytes 11010080 | tf_op jit(solution)/shard_map/all_to_all | solution.py:13
  456.8 8.2 %gather_fusion = bf16[16,128,1792]{2,1,0:T(8,128)(2,1)} fusion(bf16[24,128,1792]{2,1,0:T(8,128)(2,1)} %bitcast.9, s32[1024]{0:T(1024)S(1)} %pad_clamp_fusion), kind=kCustom, calls=%fused_computation | custom fusion | bytes 14680128 | tf_op jit(solution)/shard_map/jit(_take)/gather | solution.py:22
  465.0 6.9 %broadcast_select_fusion = bf16[16,128,1792]{2,1,0:T(8,128)(2,1)} fusion(bf16[16,128,1792]{2,1,0:T(8,128)(2,1)} %gather_fusion, pred[16]{0:T(512)(128)(4,1)S(1)} %get-tuple-element.5), kind=kLoop, calls=%fused_computation.2 | loop fusion | flops 3670016 | bytes 14680080 | tf_op jit(solution)/shard_map/jit(_take)/select_n | solution.py:22
  471.9 0.0 all-gather.5.cloned.1.call-update
  471.9 0.0 all-gather.3.cloned.1.call-done
  471.9 26.6 %all-gather.5.cloned.1.call-done = bf16[16,256,1792]{2,1,0:T(8,128)(2,1)} async-done(((bf16[16,128,1792]{2,1,0:T(8,128)(2,1)}), bf16[16,256,1792]{2,1,0:T(8,128)(2,1)}) %all-gather.5.cloned.1.call-update) | async-done | bytes 14680080 | tf_op jit(solution)/shard_map/all_gather | solution.py:23
  498.6 38.6 %convolution_convert_fusion = bf16[2048,1792]{1,0:T(8,128)(2,1)} fusion(bf16[2048,4096]{1,0:T(8,128)(2,1)} %all-gather.3.cloned.1.call-done, bf16[4096,1792]{1,0:T(8,128)(2,1)} %bitcast.22), kind=kOutput, calls=%fused_computation.1 | convolution fusion | flops 30068441088 | bytes 38797312 | tf_op jit(solution)/shard_map/dot_general | solution.py:41
  (4 shorter events, 0.0 us)
Async XLA Ops:
  6.5 465.4 %all-gather.3.cloned.1.call-start = ((), (), s32[]{:S(2)}) async-start(), calls=%async_computation.1 | async-start | bytes 18874368 | tf_op jit(solution)/shard_map/all_gather | solution.py:42
  31.3 7.6 %copy-start = (s32[16]{0:T(128)S(1)}, s32[16]{0:T(128)}, u32[]{:S(2)}) copy-start(s32[16]{0:T(128)} %param.5) | copy-start | bytes 196
  31.3 425.4 %all-to-all-start = ((bf16[8,3,128,1792]{3,2,1,0:T(8,128)(2,1)}), bf16[8,3,128,1792]{3,2,1,0:T(8,128)(2,1)}, u32[]{:S(2)}, u32[]{:S(2)}) async-start(bf16[8,3,128,1792]{3,2,1,0:T(8,128)(2,1)} %bitcast_dynamic-update-slice_fusion), calls=%async_computation | async-start | bytes 22020096 | tf_op jit(solution)/shard_map/all_to_all | solution.py:13
  38.9 459.7 %all-gather.5.cloned.1.call-start = ((), (), s32[]{:S(2)}) async-start(), calls=%async_computation.2 | async-start | bytes 22020096 | tf_op jit(solution)/shard_map/all_gather | solution.py:23
Sparse Core Ops, SparseCore 0:
  10.9 456.1 all-gather.2
  472.0 26.4 all-gather.4
